TPU v7x, 32 devices: a whole 2x2x4 slice. The times are simulated.
32 devices in a mesh: grp: 4 (over y, x), ta: 8 (over z, core).
Axes of the slice: x: 2, y: 2, z: 4, core: 2. Of those that a mesh axis runs over, the one named last changes fastest.
Arguments:
- gain: float32 [4096, 128, 128], P(('grp', 'ta')), as said below
- pred_mean: float32 [4096, 128], P(('grp', 'ta')), may hold values from -6 to 6
- update: float32 [4096, 128], P(('grp', 'ta')), as said below
- present: int32 [4096], P(('grp', 'ta')), may hold values 0 or 1
- step_cov: float32 [4096, 128, 128], P(('grp', 'ta')), as said below
Outputs:
- smooth_mean: float32 [4096, 128], P(('grp', 'ta'))
- smooth_cov: float32 [4096, 128, 128], P(('grp', 'ta'))
Inputs may be any that keep to these rules, and one draw needn't show every extreme that they name: gain is a dense real matrix per step. `update`: any real values. `step_cov`: each step_cov_k is symmetric positive definite.
All inputs are finite; a program needn't handle non-finite values. No bound on the sum of `present` on one device may be relied on, other than what follows from the above.
Results may differ from a plain program's by a relative error of at most 0.0003.
Values sent between devices are 32-bit elements; how exact they have to be, the bound alone decides.
A program may use at most 128 MiB of HBM per device.

v0:
```python
import functools

import jax
import jax.numpy as jnp
from jax import lax
from jax.experimental import pallas as pl
from jax.experimental.pallas import tpu as pltpu
from jax.sharding import PartitionSpec as P

AXES = ("grp", "ta")
CHAINS = 8
PAD = 16
F32, BF16 = jnp.float32, jnp.bfloat16


def halves(x):
    high = x.astype(BF16)
    low = (x - high.astype(F32)).astype(BF16)
    return high, low


def packed(x):
    return jnp.concatenate(halves(x), axis=1)


def weight_nt(g):
    high, low = halves(g)
    return jnp.concatenate(
        [jnp.concatenate([high, high], axis=1), jnp.concatenate([low, low], axis=1)], axis=0
    )


def weight_nn(g):
    row = packed(g)
    return jnp.concatenate([row, row], axis=0)


def diagonal_apart(g):
    on = lax.broadcasted_iota(jnp.int32, g.shape, 0) == lax.broadcasted_iota(jnp.int32, g.shape, 1)
    return jnp.sum(jnp.where(on, g, 0.0), axis=0, keepdims=True), jnp.where(on, 0.0, g)


def mul(x, w, dim, diagonal):
    out = lax.dot_general(packed(x), w, (((1,), (dim,)), ((), ())), preferred_element_type=F32)
    width = out.shape[1] // 2
    return out[:, :width] + out[:, width:] + x * diagonal


def advance(x, g, dim, lead, cov, extra):
    width = cov.shape[0]
    diagonal, rest = diagonal_apart(g)
    w = weight_nt(rest) if dim else weight_nn(rest)
    y = mul(x, w, dim, diagonal)
    turned = y[lead : lead + width].T
    return y[:lead], mul(turned, w, dim, diagonal) + cov, y[lead + width :] + extra


def measured(pres_ref, upd_ref, row):
    here = pres_ref[row].astype(F32) * upd_ref[pl.ds(row, 1), :]
    return jnp.broadcast_to(here, (PAD, here.shape[1]))


def is_last():
    length = lax.axis_size("ta")
    at = lax.axis_index("grp") * length + lax.axis_index("ta")
    return at == lax.axis_size("grp") * length - 1


def summary_kernel(pres_ref, g_ref, q_ref, upd_ref, out_ref):
    t = pl.program_id(0)
    chains, length = CHAINS, pl.num_programs(0)
    width = g_ref.shape[-1]
    s = length - 1 - t
    keep = jnp.where(is_last(), 0.0, 1.0).astype(F32)

    @pl.when(t == 0)
    def _():
        for b in range(chains):
            g = g_ref[b, 0]
            if b == chains - 1:
                g = g * keep
            out_ref[b, :width] = g.T
            out_ref[b, width : 2 * width] = q_ref[b, 0]
            out_ref[b, 2 * width :] = measured(pres_ref, upd_ref, b * length + s)

    @pl.when(t > 0)
    def _():
        for b in range(chains):
            g = g_ref[b, 0]
            extra = measured(pres_ref, upd_ref, b * length + s)
            lead, cov, d = advance(out_ref[b], g, 1, width, q_ref[b, 0], extra)
            out_ref[b, :width] = lead
            out_ref[b, width : 2 * width] = cov
            out_ref[b, 2 * width :] = d

    @pl.when(t == length - 1)
    def _():
        half = 1
        while half < chains:
            for first in range(0, chains, 2 * half):
                later = out_ref[first + half]
                for i in range(first, first + half):
                    own = out_ref[i]
                    lead, cov, d = advance(
                        later, own[:width], 0, width, own[width : 2 * width], own[2 * width :]
                    )
                    out_ref[i, :width] = lead
                    out_ref[i, width : 2 * width] = cov
                    out_ref[i, 2 * width :] = d
            half *= 2


def apply_kernel(pres_ref, g_ref, q_ref, upd_ref, pm_ref, suffix_ref, carry_ref, mean_ref, cov_ref, state):
    t = pl.program_id(0)
    chains, length = CHAINS, pl.num_programs(0)
    width = g_ref.shape[-1]
    s = length - 1 - t

    @pl.when(t == 0)
    def _():
        state[chains - 1] = jnp.where(is_last(), 0.0, carry_ref[...])
        for b in range(chains - 1):
            own = suffix_ref[b + 1]
            unused, cov, d = advance(
                carry_ref[...], own[:width], 0, 0, own[width : 2 * width], own[2 * width :]
            )
            state[b, :width] = cov
            state[b, width:] = d

    for b in range(chains):
        g = g_ref[b, 0]
        if b == chains - 1:
            g = g * jnp.where(is_last() & (t == 0), 0.0, 1.0).astype(F32)
        row = b * length + s
        unused, cov, d = advance(
            state[b], g, 1, 0, q_ref[b, 0], measured(pres_ref, upd_ref, row)
        )
        state[b, :width] = cov
        state[b, width:] = d
        cov_ref[b, 0] = cov
        mean_ref[pl.ds(row, 1), :] = pm_ref[pl.ds(row, 1), :] + d[:1]


def compose(own, later, width):
    exact = lax.Precision.HIGHEST
    turned = own[:width]
    y = jnp.matmul(later, turned, precision=exact)
    cov = jnp.matmul(y[width : 2 * width].T, turned, precision=exact) + own[width : 2 * width]
    return jnp.concatenate([y[:width], cov, y[2 * width :] + own[2 * width :]])


def moved(x, by):
    size = lax.axis_size(AXES)
    return lax.ppermute(x, AXES, [(i + by, i) for i in range(size - by)])


def body(gain, pred_mean, update, present, step_cov):
    steps, width = pred_mean.shape
    length = steps // CHAINS
    rows = 2 * width + PAD
    gain = gain.reshape(CHAINS, length, width, width)
    step_cov = step_cov.reshape(CHAINS, length, width, width)
    smem = pl.BlockSpec(memory_space=pltpu.SMEM)
    stream = pl.BlockSpec((CHAINS, 1, width, width), lambda t: (0, length - 1 - t, 0, 0))

    def fixed(*shape):
        return pl.BlockSpec(shape, lambda t: (0,) * len(shape))

    suffix = pl.pallas_call(
        summary_kernel,
        grid=(length,),
        in_specs=[smem, stream, stream, fixed(steps, width)],
        out_specs=fixed(CHAINS, rows, width),
        out_shape=jax.ShapeDtypeStruct((CHAINS, rows, width), F32),
        compiler_params=pltpu.CompilerParams(vmem_limit_bytes=40 << 20),
    )(present, gain, step_cov, update)

    total = suffix[0]
    size = lax.axis_size(AXES)
    by = 1
    while 2 * by < size:
        total = compose(total, moved(total, by), width)
        by *= 2
    near, far = moved(total, 1), moved(total, by + 1)
    carry = compose(near, far, width)[width:]

    mean, cov = pl.pallas_call(
        apply_kernel,
        grid=(length,),
        in_specs=[smem, stream, stream, fixed(steps, width), fixed(steps, width),
                  fixed(CHAINS, rows, width), fixed(width + PAD, width)],
        out_specs=[fixed(steps, width), stream],
        out_shape=[
            jax.ShapeDtypeStruct((steps, width), F32),
            jax.ShapeDtypeStruct((CHAINS, length, width, width), F32),
        ],
        scratch_shapes=[pltpu.VMEM((CHAINS, width + PAD, width), F32)],
        compiler_params=pltpu.CompilerParams(vmem_limit_bytes=40 << 20),
    )(present, gain, step_cov, update, pred_mean, suffix, carry)
    return mean, cov.reshape(steps, width, width)


def solution(mesh):
    placed = (P(AXES, None, None), P(AXES, None), P(AXES, None), P(AXES), P(AXES, None, None))
    return jax.shard_map(
        body,
        mesh=mesh,
        in_specs=placed,
        out_specs=(P(AXES, None), P(AXES, None, None)),
        check_vma=False,
    )
```

profile of v0, /device:TPU:2, one launch (start us, length us, event | category | flops | bytes accessed | tf_op | source)
XLA Modules:
  0.0 119.3 jit_solution(16279271384576362493)
XLA Ops:
  0.6 0.0 copy-start
  0.6 3.4 %copy-done = f32[128,128,128]{2,1,0:T(8,128)S(1)} copy-done((f32[128,128,128]{2,1,0:T(8,128)S(1)}, f32[128,128,128]{2,1,0:T(8,128)}, u32[]{:S(2)}) %copy-start) | copy-done | bytes 8388632
  4.0 0.0 copy-start.1
  4.0 0.8 copy-done.1
  4.9 0.0 copy-start.3
  4.9 0.7 copy-done.3
  5.5 43.8 %shard_map.68.suffix_ref = f32[8,272,128]{2,1,0:T(8,128)S(1)} custom-call(s32[128]{0:T(128)S(1)} %copy-done.3, f32[8,16,128,128]{3,2,1,0:T(8,128)S(1)} %bitcast.22, f32[8,16,128,128]{3,2,1,0:T(8,128)} %bitcast.24, f32[128,128]{1,0:T(8,128)S(1)} %copy-done.1), custom_call_target="tpu_custom_call" | custom-call | tf_op jit(solution)/shard_map/pallas_call | solution.py:169
  49.4 4.9 %collective-permute-start = (f32[272,128]{1,0:T(8,128)S(1)}, f32[272,128]{1,0:T(8,128)S(1)}, u32[]{:S(2)}, u32[]{:S(2)}) collective-permute-start(f32[272,128]{1,0:T(8,128)S(1)} %slice_bitcast_fusion), channel_id=1, source_target_pairs={{1,0},{2,1},{3,2},{4,3},{5,4},{6,5},{7,6},{8,7},{9,8},{10,9},{11,1... | collective-permute-start | bytes 417800 | tf_op jit(solution)/shard_map/ppermute | solution.py:154
  54.3 2.6 %collective-permute-done = f32[272,128]{1,0:T(8,128)S(1)} collective-permute-done((f32[272,128]{1,0:T(8,128)S(1)}, f32[272,128]{1,0:T(8,128)S(1)}, u32[]{:S(2)}, u32[]{:S(2)}) %collective-permute-start) | collective-permute-done | bytes 139296 | tf_op jit(solution)/shard_map/ppermute | solution.py:154
  56.9 0.3 fusion.5
  57.2 0.3 convolution_add_fusion.4
  57.5 2.5 %collective-permute-start.1 = (f32[272,128]{1,0:T(8,128)S(1)}, f32[272,128]{1,0:T(8,128)S(1)}, u32[]{:S(2)}, u32[]{:S(2)}) collective-permute-start(f32[272,128]{1,0:T(8,128)S(1)} %pad_maximum_fusion), channel_id=1, source_target_pairs={{2,0},{3,1},{4,2},{5,3},{6,4},{7,5},{8,6},{9,7},{10,8},{11,9},{12,... | collective-permute-start | bytes 417800 | tf_op jit(solution)/shard_map/ppermute | solution.py:154
  60.0 4.5 %collective-permute-done.1 = f32[272,128]{1,0:T(8,128)S(1)} collective-permute-done((f32[272,128]{1,0:T(8,128)S(1)}, f32[272,128]{1,0:T(8,128)S(1)}, u32[]{:S(2)}, u32[]{:S(2)}) %collective-permute-start.1) | collective-permute-done | bytes 139296 | tf_op jit(solution)/shard_map/ppermute | solution.py:154
  64.4 0.3 fusion.17
  64.7 0.3 convolution_add_fusion.3
  65.0 1.9 %collective-permute-start.2 = (f32[272,128]{1,0:T(8,128)S(1)}, f32[272,128]{1,0:T(8,128)S(1)}, u32[]{:S(2)}, u32[]{:S(2)}) collective-permute-start(f32[272,128]{1,0:T(8,128)S(1)} %pad_maximum_fusion.1), channel_id=1, source_target_pairs={{4,0},{5,1},{6,2},{7,3},{8,4},{9,5},{10,6},{11,7},{12,8},{13,9},{1... | collective-permute-start | bytes 417800 | tf_op jit(solution)/shard_map/ppermute | solution.py:154
  67.0 8.2 %collective-permute-done.2 = f32[272,128]{1,0:T(8,128)S(1)} collective-permute-done((f32[272,128]{1,0:T(8,128)S(1)}, f32[272,128]{1,0:T(8,128)S(1)}, u32[]{:S(2)}, u32[]{:S(2)}) %collective-permute-start.2) | collective-permute-done | bytes 139296 | tf_op jit(solution)/shard_map/ppermute | solution.py:154
  75.2 0.3 fusion.14
  75.5 0.3 convolution_add_fusion.2
  75.8 0.0 copy-start.2
  75.8 1.9 %collective-permute-start.3 = (f32[272,128]{1,0:T(8,128)S(1)}, f32[272,128]{1,0:T(8,128)S(1)}, u32[]{:S(2)}, u32[]{:S(2)}) collective-permute-start(f32[272,128]{1,0:T(8,128)S(1)} %pad_maximum_fusion.2), channel_id=1, source_target_pairs={{8,0},{9,1},{10,2},{11,3},{12,4},{13,5},{14,6},{15,7},{16,8},{17,9... | collective-permute-start | bytes 417800 | tf_op jit(solution)/shard_map/ppermute | solution.py:154
  77.8 7.7 %collective-permute-done.3 = f32[272,128]{1,0:T(8,128)S(1)} collective-permute-done((f32[272,128]{1,0:T(8,128)S(1)}, f32[272,128]{1,0:T(8,128)S(1)}, u32[]{:S(2)}, u32[]{:S(2)}) %collective-permute-start.3) | collective-permute-done | bytes 139296 | tf_op jit(solution)/shard_map/ppermute | solution.py:154
  85.4 0.3 fusion.11
  85.7 0.3 convolution_add_fusion.1
  86.0 4.1 %collective-permute-start.5 = (f32[272,128]{1,0:T(8,128)S(1)}, f32[272,128]{1,0:T(8,128)S(1)}, u32[]{:S(2)}, u32[]{:S(2)}) collective-permute-start(f32[272,128]{1,0:T(8,128)S(1)} %pad_maximum_fusion.3), channel_id=1, source_target_pairs={{1,0},{2,1},{3,2},{4,3},{5,4},{6,5},{7,6},{8,7},{9,8},{10,9},{11,1... | collective-permute-start | bytes 417800 | tf_op jit(solution)/shard_map/ppermute | solution.py:154
  90.2 1.3 %collective-permute-start.4 = (f32[272,128]{1,0:T(8,128)S(1)}, f32[272,128]{1,0:T(8,128)S(1)}, u32[]{:S(2)}, u32[]{:S(2)}) collective-permute-start(f32[272,128]{1,0:T(8,128)S(1)} %pad_maximum_fusion.3), channel_id=1, source_target_pairs={{17,0},{18,1},{19,2},{20,3},{21,4},{22,5},{23,6},{24,7},{25,8},{26... | collective-permute-start | bytes 417800 | tf_op jit(solution)/shard_map/ppermute | solution.py:154
  91.5 1.3 %collective-permute-done.5 = f32[272,128]{1,0:T(8,128)S(1)} collective-permute-done((f32[272,128]{1,0:T(8,128)S(1)}, f32[272,128]{1,0:T(8,128)S(1)}, u32[]{:S(2)}, u32[]{:S(2)}) %collective-permute-start.5) | collective-permute-done | bytes 139296 | tf_op jit(solution)/shard_map/ppermute | solution.py:154
  92.8 4.6 %collective-permute-done.4 = f32[272,128]{1,0:T(8,128)S(1)} collective-permute-done((f32[272,128]{1,0:T(8,128)S(1)}, f32[272,128]{1,0:T(8,128)S(1)}, u32[]{:S(2)}, u32[]{:S(2)}) %collective-permute-start.4) | collective-permute-done | bytes 139296 | tf_op jit(solution)/shard_map/ppermute | solution.py:154
  97.4 0.3 fusion.7
  97.7 0.3 convolution_add_fusion
  98.0 0.0 copy-done.2
  98.0 21.3 %shard_map.69 = (f32[128,128]{1,0:T(8,128)}, f32[8,16,128,128]{3,2,1,0:T(8,128)}) custom-call(s32[128]{0:T(128)S(1)} %copy-done.3, f32[8,16,128,128]{3,2,1,0:T(8,128)S(1)} %bitcast.23, f32[8,16,128,128]{3,2,1,0:T(8,128)} %bitcast.25, f32[128,128]{1,0:T(8,128)S(1)} %copy-done.1, f32[128,128]{1,0:T(8,128)S(1)} %copy-done.2, ...), custom_call_target="tpu_custom_call" | custom-call | tf_op jit(solution)/shard_map/pallas_call | solution.py:187
  (15 shorter events, 0.1 us)
Async XLA Ops:
  0.6 3.4 %copy-start = (f32[128,128,128]{2,1,0:T(8,128)S(1)}, f32[128,128,128]{2,1,0:T(8,128)}, u32[]{:S(2)}) copy-start(f32[128,128,128]{2,1,0:T(8,128)} %param.5) | copy-start | bytes 25165828
  4.0 0.8 copy-start.1
  4.9 0.7 copy-start.3
  49.4 7.5 %collective-permute-start = (f32[272,128]{1,0:T(8,128)S(1)}, f32[272,128]{1,0:T(8,128)S(1)}, u32[]{:S(2)}, u32[]{:S(2)}) collective-permute-start(f32[272,128]{1,0:T(8,128)S(1)} %slice_bitcast_fusion), channel_id=1, source_target_pairs={{1,0},{2,1},{3,2},{4,3},{5,4},{6,5},{7,6},{8,7},{9,8},{10,9},{11,1... | collective-permute-start | bytes 417800 | tf_op jit(solution)/shard_map/ppermute | solution.py:154
  57.5 6.9 %collective-permute-start.1 = (f32[272,128]{1,0:T(8,128)S(1)}, f32[272,128]{1,0:T(8,128)S(1)}, u32[]{:S(2)}, u32[]{:S(2)}) collective-permute-start(f32[272,128]{1,0:T(8,128)S(1)} %pad_maximum_fusion), channel_id=1, source_target_pairs={{2,0},{3,1},{4,2},{5,3},{6,4},{7,5},{8,6},{9,7},{10,8},{11,9},{12,... | collective-permute-start | bytes 417800 | tf_op jit(solution)/shard_map/ppermute | solution.py:154
  65.0 10.2 %collective-permute-start.2 = (f32[272,128]{1,0:T(8,128)S(1)}, f32[272,128]{1,0:T(8,128)S(1)}, u32[]{:S(2)}, u32[]{:S(2)}) collective-permute-start(f32[272,128]{1,0:T(8,128)S(1)} %pad_maximum_fusion.1), channel_id=1, source_target_pairs={{4,0},{5,1},{6,2},{7,3},{8,4},{9,5},{10,6},{11,7},{12,8},{13,9},{1... | collective-permute-start | bytes 417800 | tf_op jit(solution)/shard_map/ppermute | solution.py:154
  75.8 22.2 %copy-start.2 = (f32[128,128]{1,0:T(8,128)S(1)}, f32[128,128]{1,0:T(8,128)}, u32[]{:S(2)}) copy-start(f32[128,128]{1,0:T(8,128)} %pm_ref.1) | copy-start | bytes 196612
  75.8 9.6 %collective-permute-start.3 = (f32[272,128]{1,0:T(8,128)S(1)}, f32[272,128]{1,0:T(8,128)S(1)}, u32[]{:S(2)}, u32[]{:S(2)}) collective-permute-start(f32[272,128]{1,0:T(8,128)S(1)} %pad_maximum_fusion.2), channel_id=1, source_target_pairs={{8,0},{9,1},{10,2},{11,3},{12,4},{13,5},{14,6},{15,7},{16,8},{17,9... | collective-permute-start | bytes 417800 | tf_op jit(solution)/shard_map/ppermute | solution.py:154
  86.0 6.7 %collective-permute-start.5 = (f32[272,128]{1,0:T(8,128)S(1)}, f32[272,128]{1,0:T(8,128)S(1)}, u32[]{:S(2)}, u32[]{:S(2)}) collective-permute-start(f32[272,128]{1,0:T(8,128)S(1)} %pad_maximum_fusion.3), channel_id=1, source_target_pairs={{1,0},{2,1},{3,2},{4,3},{5,4},{6,5},{7,6},{8,7},{9,8},{10,9},{11,1... | collective-permute-start | bytes 417800 | tf_op jit(solution)/shard_map/ppermute | solution.py:154
  90.2 7.2 %collective-permute-start.4 = (f32[272,128]{1,0:T(8,128)S(1)}, f32[272,128]{1,0:T(8,128)S(1)}, u32[]{:S(2)}, u32[]{:S(2)}) collective-permute-start(f32[272,128]{1,0:T(8,128)S(1)} %pad_maximum_fusion.3), channel_id=1, source_target_pairs={{17,0},{18,1},{19,2},{20,3},{21,4},{22,5},{23,6},{24,7},{25,8},{26... | collective-permute-start | bytes 417800 | tf_op jit(solution)/shard_map/ppermute | solution.py:154
where the time goes:
time: 120 us; the launch traced here: 119 us
  Pallas kernels  65.1 us (54%)
  waiting for transfers between devices  28.9 us (24%)
  starting transfers between devices  16.7 us (14%)
  local copies, waits for them, and re-layouts  4.91 us (4%)
  matrix products  2.75 us (2%)
    pallas_call x1, Pallas kernels, body(): pl.pallas_call(summary_kernel, grid=(length,), in_specs=[smem, stream, st...  43.8 us
    ppermute x6, waiting for transfers between devices, moved(): return lax.ppermute(x, AXES, [(i + by, i) for i in range(size - by)])  28.9 us
    pallas_call x1, Pallas kernels, body(): pl.pallas_call(apply_kernel, grid=(length,), in_specs=[smem, stream, stre...  21.3 us
    ppermute x6, starting transfers between devices, moved(): return lax.ppermute(x, AXES, [(i + by, i) for i in range(size - by)])  16.7 us
    unnamed x8, local copies, waits for them, and re-layouts  4.87 us
  transfers between devices with their start and end apart: 6, of which 6 were waited for; matrix products, arithmetic and copies ran while one was open for 0% of the time, Pallas kernels for 0%

commit v1 on v0

--- a/solution.py
+++ b/solution.py
@@ -8,8 +8,10 @@
 from jax.sharding import PartitionSpec as P
 
 AXES = ("grp", "ta")
-CHAINS = 8
+CHAINS = 16
+GROUP = 16
 PAD = 16
+LIMIT = 60 << 20
 F32, BF16 = jnp.float32, jnp.bfloat16
 
 
@@ -46,11 +48,15 @@
     return out[:, :width] + out[:, width:] + x * diagonal
 
 
-def advance(x, g, dim, lead, cov, extra):
-    width = cov.shape[0]
+def begin(x, g, dim):
     diagonal, rest = diagonal_apart(g)
     w = weight_nt(rest) if dim else weight_nn(rest)
-    y = mul(x, w, dim, diagonal)
+    return mul(x, w, dim, diagonal), w, diagonal
+
+
+def finish(begun, dim, lead, cov, extra):
+    y, w, diagonal = begun
+    width = cov.shape[0]
     turned = y[lead : lead + width].T
     return y[:lead], mul(turned, w, dim, diagonal) + cov, y[lead + width :] + extra
 
@@ -85,28 +91,36 @@
 
     @pl.when(t > 0)
     def _():
-        for b in range(chains):
-            g = g_ref[b, 0]
-            extra = measured(pres_ref, upd_ref, b * length + s)
-            lead, cov, d = advance(out_ref[b], g, 1, width, q_ref[b, 0], extra)
-            out_ref[b, :width] = lead
-            out_ref[b, width : 2 * width] = cov
-            out_ref[b, 2 * width :] = d
+        for group in range(0, chains, GROUP):
+            members = range(group, group + GROUP)
+            begun = [begin(out_ref[b], g_ref[b, 0], 1) for b in members]
+            done = [
+                finish(ahead, 1, width, q_ref[b, 0], measured(pres_ref, upd_ref, b * length + s))
+                for b, ahead in zip(members, begun)
+            ]
+            for b, (lead, cov, d) in zip(members, done):
+                out_ref[b, :width] = lead
+                out_ref[b, width : 2 * width] = cov
+                out_ref[b, 2 * width :] = d
 
     @pl.when(t == length - 1)
     def _():
         half = 1
         while half < chains:
-            for first in range(0, chains, 2 * half):
-                later = out_ref[first + half]
-                for i in range(first, first + half):
-                    own = out_ref[i]
-                    lead, cov, d = advance(
-                        later, own[:width], 0, width, own[width : 2 * width], own[2 * width :]
-                    )
-                    out_ref[i, :width] = lead
-                    out_ref[i, width : 2 * width] = cov
-                    out_ref[i, 2 * width :] = d
+            pairs = [
+                (i, first + half)
+                for first in range(0, chains, 2 * half)
+                for i in range(first, first + half)
+            ]
+            begun = [begin(out_ref[later], out_ref[i, :width], 0) for i, later in pairs]
+            done = [
+                finish(ahead, 0, width, out_ref[i, width : 2 * width], out_ref[i, 2 * width :])
+                for (i, later), ahead in zip(pairs, begun)
+            ]
+            for (i, later), (lead, cov, d) in zip(pairs, done):
+                out_ref[i, :width] = lead
+                out_ref[i, width : 2 * width] = cov
+                out_ref[i, 2 * width :] = d
             half *= 2
 
 
@@ -119,39 +133,107 @@
     @pl.when(t == 0)
     def _():
         state[chains - 1] = jnp.where(is_last(), 0.0, carry_ref[...])
-        for b in range(chains - 1):
-            own = suffix_ref[b + 1]
-            unused, cov, d = advance(
-                carry_ref[...], own[:width], 0, 0, own[width : 2 * width], own[2 * width :]
-            )
+        begun = [begin(carry_ref[...], suffix_ref[b, :width], 0) for b in range(1, chains)]
+        done = [
+            finish(ahead, 0, 0, suffix_ref[b + 1, width : 2 * width], suffix_ref[b + 1, 2 * width :])
+            for b, ahead in enumerate(begun)
+        ]
+        for b, (unused, cov, d) in enumerate(done):
             state[b, :width] = cov
             state[b, width:] = d
 
-    for b in range(chains):
-        g = g_ref[b, 0]
-        if b == chains - 1:
-            g = g * jnp.where(is_last() & (t == 0), 0.0, 1.0).astype(F32)
-        row = b * length + s
-        unused, cov, d = advance(
-            state[b], g, 1, 0, q_ref[b, 0], measured(pres_ref, upd_ref, row)
+    keep = jnp.where(is_last() & (t == 0), 0.0, 1.0).astype(F32)
+    for group in range(0, chains, GROUP):
+        members = range(group, group + GROUP)
+        begun = []
+        for b in members:
+            g = g_ref[b, 0]
+            begun.append(begin(state[b], g * keep if b == chains - 1 else g, 1))
+        done = [
+            finish(ahead, 1, 0, q_ref[b, 0], measured(pres_ref, upd_ref, b * length + s))
+            for b, ahead in zip(members, begun)
+        ]
+        for b, (unused, cov, d) in zip(members, done):
+            row = b * length + s
+            state[b, :width] = cov
+            state[b, width:] = d
+            cov_ref[b, 0] = cov
+            mean_ref[pl.ds(row, 1), :] = pm_ref[pl.ds(row, 1), :] + d[:1]
+
+
+def distances(size):
+    by, rounds = 1, []
+    while 2 * by < size:
+        rounds.append(by)
+        by *= 2
+    return rounds, by + 1
+
+
+def exchange_kernel(total_ref, carry_ref, held, got, far, sems):
+    width = total_ref.shape[1]
+    inner = lax.axis_size("ta")
+    size = lax.axis_size("grp") * inner
+    me = lax.axis_index("grp") * inner + lax.axis_index("ta")
+    rounds, reach = distances(size)
+    lead, rest = pl.ds(0, width), pl.ds(width, width + PAD)
+
+    def device(offset):
+        at = lax.rem(me + offset, size)
+        return (at // inner, lax.rem(at, inner))
+
+    barrier = pltpu.get_barrier_semaphore()
+    offsets = sorted({o % size for by in rounds + [1, reach] for o in (by, -by)})
+    for offset in offsets:
+        pl.semaphore_signal(barrier, inc=1, device_id=device(offset), device_id_type=pl.DeviceIdType.MESH)
+    pl.semaphore_wait(barrier, len(offsets))
+
+    def send(source, target, sem, by):
+        copy = pltpu.make_async_remote_copy(
+            src_ref=source,
+            dst_ref=target,
+            send_sem=sems.at[sem, 0],
+            recv_sem=sems.at[sem, 1],
+            device_id=device(size - by),
+            device_id_type=pl.DeviceIdType.MESH,
         )
-        state[b, :width] = cov
-        state[b, width:] = d
-        cov_ref[b, 0] = cov
-        mean_ref[pl.ds(row, 1), :] = pm_ref[pl.ds(row, 1), :] + d[:1]
-
-
-def compose(own, later, width):
-    exact = lax.Precision.HIGHEST
-    turned = own[:width]
-    y = jnp.matmul(later, turned, precision=exact)
-    cov = jnp.matmul(y[width : 2 * width].T, turned, precision=exact) + own[width : 2 * width]
-    return jnp.concatenate([y[:width], cov, y[2 * width :] + own[2 * width :]])
-
-
-def moved(x, by):
-    size = lax.axis_size(AXES)
-    return lax.ppermute(x, AXES, [(i + by, i) for i in range(size - by)])
+        copy.start()
+        return copy
+
+    def received(copy, ref, by):
+        copy.wait_recv()
+        return jnp.where(me + by < size, ref[...], 0.0)
+
+    hops = rounds + [1]
+    last = len(rounds)
+    held[0] = total_ref[...]
+    first = send(held.at[0, lead], got.at[0, lead], 0, hops[0])
+    second = send(held.at[0, rest], got.at[0, rest], 1, hops[0])
+    sent = [first, second]
+    for r, by in enumerate(rounds):
+        turned = held[r, :width]
+        diagonal, others = diagonal_apart(turned)
+        w = weight_nn(others)
+        joined = mul(received(first, got.at[r, lead], by), w, 0, diagonal)
+        held[r + 1, :width] = joined
+        first = send(held.at[r + 1, lead], got.at[r + 1, lead], 2 * r + 2, hops[r + 1])
+        sent.append(first)
+        y = mul(received(second, got.at[r, rest], by), w, 0, diagonal)
+        held[r + 1, width : 2 * width] = mul(y[:width].T, w, 0, diagonal) + held[r, width : 2 * width]
+        held[r + 1, 2 * width :] = y[width:] + held[r, 2 * width :]
+        second = send(held.at[r + 1, rest], got.at[r + 1, rest], 2 * r + 3, hops[r + 1])
+        sent.append(second)
+        if r == last - 1:
+            third = send(held.at[last, rest], far, 2 * last + 2, reach)
+            sent.append(third)
+    turned = received(first, got.at[last, lead], 1)
+    diagonal, others = diagonal_apart(turned)
+    w = weight_nn(others)
+    y = mul(received(third, far, reach), w, 0, diagonal)
+    near = received(second, got.at[last, rest], 1)
+    carry_ref[:width] = mul(y[:width].T, w, 0, diagonal) + near[:width]
+    carry_ref[width:] = y[width:] + near[width:]
+    for copy in sent:
+        copy.wait_send()
 
 
 def body(gain, pred_mean, update, present, step_cov):
@@ -172,17 +254,26 @@
         in_specs=[smem, stream, stream, fixed(steps, width)],
         out_specs=fixed(CHAINS, rows, width),
         out_shape=jax.ShapeDtypeStruct((CHAINS, rows, width), F32),
-        compiler_params=pltpu.CompilerParams(vmem_limit_bytes=40 << 20),
+        compiler_params=pltpu.CompilerParams(vmem_limit_bytes=LIMIT),
     )(present, gain, step_cov, update)
 
-    total = suffix[0]
-    size = lax.axis_size(AXES)
-    by = 1
-    while 2 * by < size:
-        total = compose(total, moved(total, by), width)
-        by *= 2
-    near, far = moved(total, 1), moved(total, by + 1)
-    carry = compose(near, far, width)[width:]
+    rounds = len(distances(lax.axis_size(AXES))[0])
+    carry = pl.pallas_call(
+        exchange_kernel,
+        grid=(1,),
+        in_specs=[pl.BlockSpec((pl.squeezed, rows, width), lambda t: (0, 0, 0))],
+        out_specs=fixed(width + PAD, width),
+        out_shape=jax.ShapeDtypeStruct((width + PAD, width), F32),
+        scratch_shapes=[
+            pltpu.VMEM((rounds + 1, rows, width), F32),
+            pltpu.VMEM((rounds + 1, rows, width), F32),
+            pltpu.VMEM((width + PAD, width), F32),
+            pltpu.SemaphoreType.DMA((2 * rounds + 3, 2)),
+        ],
+        compiler_params=pltpu.CompilerParams(
+            collective_id=0, has_side_effects=True, vmem_limit_bytes=LIMIT
+        ),
+    )(suffix)
 
     mean, cov = pl.pallas_call(
         apply_kernel,
@@ -195,7 +286,7 @@
             jax.ShapeDtypeStruct((CHAINS, length, width, width), F32),
         ],
         scratch_shapes=[pltpu.VMEM((CHAINS, width + PAD, width), F32)],
-        compiler_params=pltpu.CompilerParams(vmem_limit_bytes=40 << 20),
+        compiler_params=pltpu.CompilerParams(vmem_limit_bytes=LIMIT),
     )(present, gain, step_cov, update, pred_mean, suffix, carry)
     return mean, cov.reshape(steps, width, width)
 

time: 120 us -> 67.9 us (0.57)
  the two profiles are of different devices: /device:TPU:2 before, /device:TPU:17 now
where the time goes in v1:
time: 67.9 us; the launch traced here: 67.4 us
  Pallas kernels  66.8 us (98%)
    pallas_call x1, Pallas kernels, body(): pl.pallas_call(exchange_kernel, grid=(1,), in_specs=[pl.BlockSpec((pl.squ...  32 us
    pallas_call x1, Pallas kernels, body(): pl.pallas_call(apply_kernel, grid=(length,), in_specs=[smem, stream, stre...  17.9 us
    pallas_call x1, Pallas kernels, body(): pl.pallas_call(summary_kernel, grid=(length,), in_specs=[smem, stream, st...  16.9 us

profile of v1, /device:TPU:17, one launch (start us, length us, event | category | flops | bytes accessed | tf_op | source)
XLA Modules:
  0.0 67.4 jit_solution(17022283090922578385)
XLA Ops:
  0.6 16.9 %shard_map.68.total_ref.suffix_ref = f32[16,272,128]{2,1,0:T(8,128)} custom-call(s32[128]{0:T(128)} %pres_ref.3, f32[16,8,128,128]{3,2,1,0:T(8,128)} %bitcast.3, f32[16,8,128,128]{3,2,1,0:T(8,128)} %bitcast.5, f32[128,128]{1,0:T(8,128)} %upd_ref.3), custom_call_target="tpu_custom_call" | custom-call | tf_op jit(solution)/shard_map/pallas_call | solution.py:251
  17.5 32.0 %shard_map.69.carry_ref = f32[144,128]{1,0:T(8,128)} custom-call(f32[16,272,128]{2,1,0:T(8,128)} %shard_map.68.total_ref.suffix_ref), custom_call_target="tpu_custom_call" | custom-call | tf_op jit(solution)/shard_map/pallas_call | solution.py:261
  49.5 17.9 %shard_map.70 = (f32[128,128]{1,0:T(8,128)}, f32[16,8,128,128]{3,2,1,0:T(8,128)}) custom-call(s32[128]{0:T(128)} %pres_ref.3, f32[16,8,128,128]{3,2,1,0:T(8,128)} %bitcast.4, f32[16,8,128,128]{3,2,1,0:T(8,128)} %bitcast.6, f32[128,128]{1,0:T(8,128)} %upd_ref.3, f32[128,128]{1,0:T(8,128)} %pm_ref.1, f32[16,272,128]{2,1,0:T(8,128)} %shard_map.68.total_ref.suffix_ref, ...), custom_call_target="tpu_custom_call" | custom-call | tf_op jit(solution)/shard_map/pallas_call | solution.py:278
